TPU v7x, 256 devices: a whole 4x4x8 slice. The times are simulated.
256 devices in a mesh: prompt: 2 (over y_lo), tm: 16 (over x, y_hi, core), head: 8 (over z).
Axes of the slice: x: 4, y: 4 (y_hi: 2, y_lo: 2; y = y_hi * 2 + y_lo), z: 8, core: 2. Of those that a mesh axis runs over, the one named last changes fastest.
Arguments:
- queries: bfloat16 [49152, 3072], P(('prompt', 'tm'), 'head'), parts along dimension 0, may hold values from -11 to 11
- key_rows: bfloat16 [49152, 3072], P(('prompt', 'tm'), 'head'), parts along dimension 0, may hold values from -11 to 11
- values: bfloat16 [49152, 3072], P(('prompt', 'tm'), 'head'), parts along dimension 0, may hold values from -24 to 24
- out_weight: bfloat16 [3072, 3072], P('head'), may hold values from -0.109375 to 0.109375
- gate_scale: float32 [6144], P('prompt'), parts along dimension 0, may hold values from 0.5 to 2
- window: int32 [256, 8, 3], P(('prompt', 'tm')), parts along dimension 0, may hold values from -1 to 1, as said below
Outputs:
- layer_out: float32 [49152, 3072], P(('prompt', 'tm', 'head')), parts along dimension 0
There are 2 independent parts, one for each index of `prompt`. A program takes and returns all parts, laid end to end along the dimension named above; an argument that names none is the same for every part. Nothing has to cross between parts.
Inputs may be any that keep to these rules, and one draw needn't show every extreme that they name: `window`: for each query tile the 8 offsets are distinct triples of -1, 0 and 1; the first is (0, 0, 0), the second has time offset 1 and the third time offset -1.
All inputs are finite; a program needn't handle non-finite values.
Results may differ from a plain program's by a relative error of at most 0.019.
Values may be sent and summed in bfloat16 or wider, within the bound.
A program may use at most 64 MiB of HBM per device.

v0:
```python
import functools
import math

import jax
import jax.numpy as jnp
from jax import lax
from jax.experimental import pallas as pl
from jax.experimental.pallas import tpu as pltpu
from jax.sharding import PartitionSpec as P

HD = 128
TILE = 192
NTH = 2
NTW = 4
SLOTS = 8
STAGGER = 4
MESH = pl.DeviceIdType.MESH
NEG = -1e30


def kernel(n_tm, n_head, n_local, q_hbm, k_hbm, v_hbm, w_hbm, window, out_hbm,
           qbuf, att, arecv, wbuf, acc, *rest):
    kbufs, vbufs = rest[:n_local], rest[n_local:2 * n_local]
    (loc_sem, out_sem, halo_send, halo_recv, core_send, core_recv, a_send, a_recv,
     ring_send, ring_recv, mate_send, mate_recv, pair_send, pair_recv) = rest[2 * n_local:]
    tokens = q_hbm.shape[0]
    tiles = tokens // TILE
    width = w_hbm.shape[1]
    half, quarter = width // 2, width // 4

    tm = lax.axis_index("tm")
    z = lax.axis_index("head")
    core = tm % 2
    x = tm // 4
    n_x = n_tm // 4
    parity = x % 2
    partner = {"tm": tm + 1 - 2 * core}
    far = {"tm": (tm - 1 + 2 * core + n_tm) % n_tm}
    below = {"tm": ((x + n_x - 1) % n_x) * 4 + tm % 4}
    above = {"tm": ((x + 1) % n_x) * 4 + tm % 4}
    mates = (
        {"tm": ((x + 1 - 2 * parity + n_x) % n_x) * 4 + tm % 4},
        {"tm": ((x - 1 + 2 * parity + n_x) % n_x) * 4 + tm % 4},
    )

    barrier = pltpu.get_barrier_semaphore()
    peers = [partner, far, below, above] + [{"head": (z + d) % n_head} for d in range(1, n_head)]
    for peer in peers:
        pl.semaphore_signal(barrier, inc=1, device_id=peer, device_id_type=MESH)

    def own_weight(h):
        return pltpu.make_async_copy(
            w_hbm.at[pl.ds(h * HD, HD)], wbuf.at[h, z], loc_sem.at[h])

    def own_kv(h):
        columns = pl.ds(h * HD, HD)
        return [
            pltpu.make_async_copy(k_hbm.at[:, :, columns], kbufs[h].at[pl.ds(0, tiles)], loc_sem.at[n_local + 2 * h]),
            pltpu.make_async_copy(v_hbm.at[:, :, columns], vbufs[h].at[pl.ds(0, tiles)], loc_sem.at[n_local + 2 * h + 1]),
        ]

    own_q = pltpu.make_async_copy(q_hbm, qbuf, loc_sem.at[3 * n_local])
    for h in range(n_local):
        own_weight(h).start()
    own_q.start()
    for h in range(n_local):
        for copy in own_kv(h):
            copy.start()

    def kv_send(h, slab, to, send, recv):
        columns = pl.ds(h * HD, HD)
        rows = pl.ds(slab * tiles, tiles)
        return [
            pltpu.make_async_remote_copy(
                src_ref=src.at[:, :, columns], dst_ref=dst.at[rows], send_sem=send.at[2 * h + i],
                recv_sem=recv.at[2 * h + i], device_id=to, device_id_type=MESH)
            for i, (src, dst) in enumerate(((k_hbm, kbufs[h]), (v_hbm, vbufs[h])))
        ]

    def far_copies(h):
        return kv_send(h, 2, far, halo_send, halo_recv)

    def core_copies(h):
        return kv_send(h, 1, partner, core_send, core_recv)

    def piece(h, block, ring, rows):
        return wbuf.at[h, block, rows, pl.ds(core * half + ring * quarter, quarter)]

    my_rows = pl.ds(parity * (HD // 2), HD // 2)

    def ring_copy(h, s, ring):
        sign = 1 - 2 * ring
        ref = piece(h, (z - sign * s + n_head) % n_head, ring, my_rows)
        return pltpu.make_async_remote_copy(
            src_ref=ref, dst_ref=ref, send_sem=ring_send.at[h, s, ring], recv_sem=ring_recv.at[h, s, ring],
            device_id={"head": (z + sign + n_head) % n_head}, device_id_type=MESH)

    def mate_copy(h, s, ring):
        sign = 1 - 2 * ring
        ref = piece(h, (z - sign * (s + 1) + 2 * n_head) % n_head, ring, my_rows)
        return pltpu.make_async_remote_copy(
            src_ref=ref, dst_ref=ref, send_sem=mate_send.at[h, s, ring], recv_sem=mate_recv.at[h, s, ring],
            device_id=mates[ring], device_id_type=MESH)

    def pair_copy(h, s, ring):
        sign = 1 - 2 * ring
        ref = piece(h, (z - sign * (s + 1) + 2 * n_head) % n_head, ring, pl.ds(0, HD))
        return pltpu.make_async_remote_copy(
            src_ref=ref, dst_ref=ref, send_sem=pair_send.at[h, s, ring], recv_sem=pair_recv.at[h, s, ring],
            device_id=partner, device_id_type=MESH)

    hops = n_head - 1

    def tick(t):
        for h in range(n_local):
            s = t - STAGGER * h
            for ring in range(2):
                if s == 0:
                    if ring == 0:
                        own_weight(h).wait()
                    ring_copy(h, 0, ring).start()
                if 1 <= s <= hops:
                    ring_copy(h, s - 1, ring).wait_recv()
                    if s < hops:
                        ring_copy(h, s, ring).start()
                    mate_copy(h, s - 1, ring).start()
            for ring in range(2):
                if 2 <= s <= hops + 1:
                    mate_copy(h, s - 2, ring).wait_recv()
                    pair_copy(h, s - 2, ring).start()

    ticks = STAGGER * (n_local - 1) + hops + 2

    factor = math.log2(math.e) / math.sqrt(HD)
    slot_of = lax.broadcasted_iota(jnp.int32, (1, SLOTS * TILE), 1) // TILE

    def a2a_copy(h, d):
        to = (z + d) % n_head
        return pltpu.make_async_remote_copy(
            src_ref=att.at[h, pl.ds(pl.multiple_of(to * TILE, TILE), TILE)],
            dst_ref=arecv.at[h, :, pl.ds(pl.multiple_of(z * HD, HD), HD)],
            send_sem=a_send.at[h, d], recv_sem=a_recv.at[h, d],
            device_id={"head": to}, device_id_type=MESH)

    def attend(h):
        kbuf, vbuf = kbufs[h], vbufs[h]

        def one_tile(step, carry):
            i = (z + 1 + step) % tiles
            i_h, i_w = i // NTW, i % NTW
            rows = pl.ds(pl.multiple_of(i * TILE, TILE), TILE)
            bias = jnp.zeros((1, SLOTS * TILE), jnp.float32)
            k_parts, v_parts = [], []
            for j in range(SLOTS):
                d_t, d_h, d_w = window[i, j, 0], window[i, j, 1], window[i, j, 2]
                t_j, h_j, w_j = tm + d_t, i_h + d_h, i_w + d_w
                valid = ((t_j >= 0) & (t_j < n_tm) & (h_j >= 0) & (h_j < NTH)
                         & (w_j >= 0) & (w_j < NTW))
                toward = d_t * (1 - 2 * core)
                slab = jnp.where(toward == 0, 0, jnp.where(toward == 1, 1, 2))
                index = jnp.where(valid, slab * tiles + h_j * NTW + w_j, i)
                bias = jnp.where(slot_of == j, jnp.where(valid, 0.0, NEG), bias)
                k_parts.append(kbuf[index])
                v_parts.append(vbuf[index])
            q = qbuf[rows, h * HD:(h + 1) * HD]
            scores = lax.dot_general(
                q, jnp.concatenate(k_parts, axis=0), (((1,), (1,)), ((), ())),
                preferred_element_type=jnp.float32) + bias
            top = jnp.max(scores, axis=1, keepdims=True)
            weights = jnp.exp2((scores - top) * factor)
            total = jnp.sum(weights, axis=1, keepdims=True)
            mixed = jnp.dot(weights.astype(jnp.bfloat16), jnp.concatenate(v_parts, axis=0),
                            preferred_element_type=jnp.float32)
            att[h, rows, :] = (mixed / total).astype(jnp.bfloat16)

            @pl.when(step < tiles - 1)
            def _():
                a2a_copy(h, step + 1).start()
            return carry

        lax.fori_loop(0, tiles, one_tile, 0)
        own_rows = pl.ds(pl.multiple_of(z * TILE, TILE), TILE)
        own_columns = pl.ds(pl.multiple_of(z * HD, HD), HD)
        arecv[h, :, own_columns] = att[h, own_rows, :]

    block = 512

    def out_copy(n):
        columns = pl.ds(n * block, block)
        return pltpu.make_async_copy(acc.at[:, columns], out_hbm.at[:, columns], out_sem.at[n])

    def project(h):
        for s in range(hops):
            for ring in range(2):
                pair_copy(h, s, ring).wait_recv()
        for d in range(1, n_head):
            a2a_copy(h, d).wait_recv()
        lhs = arecv[h]
        for n in range(width // block):
            columns = slice(n * block, (n + 1) * block)
            rhs = wbuf[h, :, :, columns].reshape(n_head * HD, block)
            term = jnp.dot(lhs, rhs, preferred_element_type=jnp.float32)
            acc[:, columns] = term if h == 0 else acc[:, columns] + term
            if h == n_local - 1:
                out_copy(n).start()

    pl.semaphore_wait(barrier, len(peers))
    for h in range(n_local):
        if h == 0:
            for copy in far_copies(h):
                copy.start()
    for h in range(n_local):
        for copy in core_copies(h):
            copy.start()

    attend_after = ATTEND_AFTER
    project_after = PROJECT_AFTER
    for t in range(ticks):
        tick(t)
        for h in range(n_local):
            if attend_after[h] == t:
                for copy in far_copies(h) + core_copies(h):
                    copy.wait_recv()
                if h + 1 < n_local:
                    for copy in far_copies(h + 1):
                        copy.start()
                for copy in own_kv(h):
                    copy.wait()
                if h == 0:
                    own_q.wait()
                attend(h)
            if project_after[h] == t:
                project(h)
    for h in range(n_local):
        for copy in far_copies(h) + core_copies(h):
            copy.wait_send()
        for d in range(1, n_head):
            a2a_copy(h, d).wait_send()
        for s in range(hops):
            for ring in range(2):
                ring_copy(h, s, ring).wait_send()
                mate_copy(h, s, ring).wait_send()
                pair_copy(h, s, ring).wait_send()
    for n in range(width // block):
        out_copy(n).wait()


ATTEND_AFTER = (4, 9, 13)
PROJECT_AFTER = (11, 15, 16)


def by_tile(rows):
    return rows.reshape(rows.shape[0] // TILE, TILE, rows.shape[1])


def body(queries, key_rows, values, out_weight, gate_scale, window):
    n_tm, n_head = lax.axis_size("tm"), lax.axis_size("head")
    tokens, features = queries.shape
    n_local = features // HD
    width = out_weight.shape[1]
    hops = n_head - 1
    dma = pltpu.SemaphoreType.DMA
    any_spec = pl.BlockSpec(memory_space=pl.ANY)
    projected = pl.pallas_call(
        functools.partial(kernel, n_tm, n_head, n_local),
        out_shape=jax.ShapeDtypeStruct((tokens // n_head, width), jnp.float32),
        in_specs=[any_spec] * 4 + [pl.BlockSpec(memory_space=pltpu.SMEM)],
        out_specs=any_spec,
        scratch_shapes=[
            pltpu.VMEM((tokens, features), jnp.bfloat16),
            pltpu.VMEM((n_local, tokens, HD), jnp.bfloat16),
            pltpu.VMEM((n_local, TILE, n_head * HD), jnp.bfloat16),
            pltpu.VMEM((n_local, n_head, HD, width), jnp.bfloat16),
            pltpu.VMEM((tokens // n_head, width), jnp.float32),
        ] + [pltpu.VMEM((3 * tokens // TILE, TILE, HD), jnp.bfloat16)] * (2 * n_local) + [
            dma((3 * n_local + 1,)), dma((width // 512,)),
            dma((2 * n_local,)), dma((2 * n_local,)), dma((2 * n_local,)), dma((2 * n_local,)),
            dma((n_local, n_head)), dma((n_local, n_head)),
            dma((n_local, hops, 2)), dma((n_local, hops, 2)),
            dma((n_local, hops, 2)), dma((n_local, hops, 2)),
            dma((n_local, hops, 2)), dma((n_local, hops, 2)),
        ],
        compiler_params=pltpu.CompilerParams(
            collective_id=0, has_side_effects=True, vmem_limit_bytes=56 << 20),
        name="attend_and_project",
    )(queries, by_tile(key_rows), by_tile(values), out_weight, window)
    return gate_scale[None, :] * projected


def solution(mesh):
    placed = (
        P(("prompt", "tm"), "head"),
        P(("prompt", "tm"), "head"),
        P(("prompt", "tm"), "head"),
        P("head", None),
        P("prompt"),
        P(("prompt", "tm"), None, None),
    )
    return jax.shard_map(
        body,
        mesh=mesh,
        in_specs=placed,
        out_specs=P(("prompt", "tm", "head"), None),
        check_vma=False,
    )
```

profile of v0, /device:TPU:1, one launch (start us, length us, event | category | flops | bytes accessed | tf_op | source)
XLA Modules:
  0.0 119.5 jit_solution(12355280258737769360)
XLA Ops:
  0.0 1.4 %copy.7.window = s32[8,8,3]{2,1,0:T(8,128)} copy(s32[8,8,3]{1,0,2:T(8,128)} %param.11) | data formatting | bytes 1536 | tf_op args[5]
  1.4 0.0 copy-start
  1.4 114.7 %attend_and_project.1 = f32[192,3072]{1,0:T(8,128)} custom-call(bf16[1536,384]{1,0:T(8,128)(2,1)} %q_hbm.1, bf16[8,192,384]{2,1,0:T(8,128)(2,1)} %bitcast.2, bf16[8,192,384]{2,1,0:T(8,128)(2,1)} %bitcast.3, bf16[384,3072]{1,0:T(8,128)(2,1)} %w_hbm.1, s32[8,8,3]{2,1,0:T(8,128)} %copy.7.window), custom_call_target="tpu_custom_call" | custom-call | tf_op jit(solution)/shard_map/attend_and_project/pallas_call | solution.py:264
  116.1 0.0 copy-done
  116.1 3.4 %broadcast_multiply_fusion = f32[192,3072]{1,0:T(8,128)} fusion(f32[192,3072]{1,0:T(8,128)} %attend_and_project.1, f32[3072]{0:T(1024)S(1)} %copy-done), kind=kLoop, calls=%fused_computation | loop fusion | flops 589824 | bytes 4730880 | tf_op jit(solution)/shard_map/mul | solution.py:287
Async XLA Ops:
  1.4 114.7 %copy-start = (f32[3072]{0:T(1024)S(1)}, f32[3072]{0:T(1024)}, u32[]{:S(2)}) copy-start(f32[3072]{0:T(1024)} %param.10) | copy-start | bytes 36868
where the time goes:
time: 120 us; the launch traced here: 119 us
  Pallas kernels  115 us (96%)
  other arithmetic  3.36 us (3%)
  local copies, waits for them, and re-layouts  1.44 us (1%)
    pallas_call x1, Pallas kernels, body(): pl.pallas_call(functools.partial(kernel, n_tm, n_head, n_local), out_shap...  115 us
    mul x1, other arithmetic, body(): return gate_scale[None, :] * projected  3.36 us

commit v1 on v0

v1 whole, which is shorter than its diff:
```python
import functools
import math

import jax
import jax.numpy as jnp
from jax import lax
from jax.experimental import pallas as pl
from jax.experimental.pallas import tpu as pltpu
from jax.sharding import PartitionSpec as P

HD = 128
TILE = 192
NTH = 2
NTW = 4
SLOTS = 8
MESH = pl.DeviceIdType.MESH
NEG = -1e30
VMEM_LIMIT = 56
FEW = 48
BUSY = 1


def kernel(n_tm, n_head, n_local, q_hbm, k_hbm, v_hbm, w_hbm, window, out,
           qbuf, att, arecv, wbuf, *rest):
    kbufs, vbufs = rest[:n_local], rest[n_local:2 * n_local]
    (loc_sem, halo_send, halo_recv, core_send, core_recv, a_send, a_recv,
     ring_send, ring_recv, mate_send, mate_recv, pair_send, pair_recv) = rest[2 * n_local:]
    tokens = q_hbm.shape[0]
    tiles = tokens // TILE
    width = w_hbm.shape[1]
    half, quarter = width // 2, width // 4

    tm = lax.axis_index("tm")
    z = lax.axis_index("head")
    core = tm % 2
    x = tm // 4
    n_x = n_tm // 4
    parity = x % 2
    partner = {"tm": tm + 1 - 2 * core}
    far = {"tm": (tm - 1 + 2 * core + n_tm) % n_tm}
    busy = (tm // 2 + BUSY + 1) % 2
    light, heavy = (
        {"tm": ((x + sign + n_x) % n_x) * 4 + tm % 4} for sign in (2 * busy - 1, 1 - 2 * busy))

    barrier = pltpu.get_barrier_semaphore()
    peers = [partner, far, light, heavy] + [{"head": (z + d) % n_head} for d in range(1, n_head)]
    for peer in peers:
        pl.semaphore_signal(barrier, inc=1, device_id=peer, device_id_type=MESH)

    def own_weight(h):
        return pltpu.make_async_copy(
            w_hbm.at[pl.ds(h * HD, HD)], wbuf.at[h, z], loc_sem.at[h])

    def own_kv(h):
        columns = pl.ds(h * HD, HD)
        return [
            pltpu.make_async_copy(k_hbm.at[:, :, columns], kbufs[h].at[pl.ds(0, tiles)], loc_sem.at[n_local + 2 * h]),
            pltpu.make_async_copy(v_hbm.at[:, :, columns], vbufs[h].at[pl.ds(0, tiles)], loc_sem.at[n_local + 2 * h + 1]),
        ]

    own_q = pltpu.make_async_copy(q_hbm, qbuf, loc_sem.at[3 * n_local])
    for h in range(n_local):
        own_weight(h).start()
    own_q.start()
    for h in range(n_local):
        for copy in own_kv(h):
            copy.start()

    def kv_send(h, slab, to, send, recv):
        columns = pl.ds(h * HD, HD)
        rows = pl.ds(slab * tiles, tiles)
        return [
            pltpu.make_async_remote_copy(
                src_ref=src.at[:, :, columns], dst_ref=dst.at[rows], send_sem=send.at[2 * h + i],
                recv_sem=recv.at[2 * h + i], device_id=to, device_id_type=MESH)
            for i, (src, dst) in enumerate(((k_hbm, kbufs[h]), (v_hbm, vbufs[h])))
        ]

    def far_copies(h):
        return kv_send(h, 2, far, halo_send, halo_recv)

    def core_copies(h):
        return kv_send(h, 1, partner, core_send, core_recv)

    counts = (FEW, HD - FEW)
    parts = ((parity + 1 - busy) % 2, (parity + busy) % 2)
    firsts = ((1 - busy) * (HD - FEW), busy * FEW)
    hops = n_head // 2

    def block_of(s, ring):
        return (z - (1 - 2 * ring) * s + n_head) % n_head

    def piece(h, block, kind):
        return wbuf.at[h, block, pl.ds(pl.multiple_of(firsts[kind], 16), counts[kind]),
                       pl.ds(pl.multiple_of(core * half + parts[kind] * quarter, HD), quarter)]

    def kinds(h, s, ring):
        return range(2) if s < hops - 1 else ((h + ring) % 2,)

    def ring_copies(h, s, ring):
        copies = []
        for kind in kinds(h, s, ring):
            ref = piece(h, block_of(s, ring), kind)
            copies.append(pltpu.make_async_remote_copy(
                src_ref=ref, dst_ref=ref, send_sem=ring_send.at[h, s, ring, kind],
                recv_sem=ring_recv.at[h, s, ring, kind],
                device_id={"head": (z + 1 - 2 * ring + n_head) % n_head}, device_id_type=MESH))
        return copies

    def mate_copies(h, s, ring):
        copies = []
        for kind in kinds(h, s, ring):
            ref = piece(h, block_of(s + 1, ring), kind)
            copies.append(pltpu.make_async_remote_copy(
                src_ref=ref, dst_ref=ref, send_sem=mate_send.at[h, s, ring, kind],
                recv_sem=mate_recv.at[h, s, ring, kind], device_id=(light, heavy)[kind], device_id_type=MESH))
        return copies

    def pair_copy(h, s, ring):
        ref = wbuf.at[h, block_of(s + 1, ring), :, pl.ds(pl.multiple_of(core * half, HD), half)]
        return pltpu.make_async_remote_copy(
            src_ref=ref, dst_ref=ref, send_sem=pair_send.at[h, s, ring], recv_sem=pair_recv.at[h, s, ring],
            device_id=partner, device_id_type=MESH)

    received = [(s, ring) for s in range(hops - 1) for ring in range(2)] + [(hops - 1, 0)]

    def tick(s):
        for h in range(n_local):
            if s == 0:
                own_weight(h).wait()
            for ring in range(2):
                if 1 <= s <= hops:
                    for copy in ring_copies(h, s - 1, ring):
                        copy.wait_recv()
                if s < hops:
                    for copy in ring_copies(h, s, ring):
                        copy.start()
                if 1 <= s <= hops:
                    for copy in mate_copies(h, s - 1, ring):
                        copy.start()

    def share(s):
        for h in range(n_local):
            for ring in range(2):
                for copy in mate_copies(h, s, ring):
                    copy.wait_recv()
                if s < hops - 1:
                    pair_copy(h, s, ring).start()
            if s == hops - 1:
                pair_copy(h, s, 0).start()

    factor = math.log2(math.e) / math.sqrt(HD)
    slot_of = lax.broadcasted_iota(jnp.int32, (1, SLOTS * TILE), 1) // TILE

    def a2a_copy(h, d):
        to = (z + d) % n_head
        return pltpu.make_async_remote_copy(
            src_ref=att.at[h, pl.ds(pl.multiple_of(to * TILE, TILE), TILE)],
            dst_ref=arecv.at[h, :, pl.ds(pl.multiple_of(z * HD, HD), HD)],
            send_sem=a_send.at[h, d], recv_sem=a_recv.at[h, d],
            device_id={"head": to}, device_id_type=MESH)

    def attend(h):
        kbuf, vbuf = kbufs[h], vbufs[h]

        def one_tile(step, carry):
            i = (z + 1 + step) % tiles
            i_h, i_w = i // NTW, i % NTW
            rows = pl.ds(pl.multiple_of(i * TILE, TILE), TILE)
            bias = jnp.zeros((1, SLOTS * TILE), jnp.float32)
            k_parts, v_parts = [], []
            for j in range(SLOTS):
                d_t, d_h, d_w = window[0, i, j], window[1, i, j], window[2, i, j]
                t_j, h_j, w_j = tm + d_t, i_h + d_h, i_w + d_w
                valid = ((t_j >= 0) & (t_j < n_tm) & (h_j >= 0) & (h_j < NTH)
                         & (w_j >= 0) & (w_j < NTW))
                toward = d_t * (1 - 2 * core)
                slab = jnp.where(toward == 0, 0, jnp.where(toward == 1, 1, 2))
                index = jnp.where(valid, slab * tiles + h_j * NTW + w_j, i)
                bias = jnp.where(slot_of == j, jnp.where(valid, 0.0, NEG), bias)
                k_parts.append(kbuf[index])
                v_parts.append(vbuf[index])
            q = qbuf[rows, h * HD:(h + 1) * HD]
            scores = lax.dot_general(
                q, jnp.concatenate(k_parts, axis=0), (((1,), (1,)), ((), ())),
                preferred_element_type=jnp.float32) + bias
            top = jnp.max(scores, axis=1, keepdims=True)
            weights = jnp.exp2((scores - top) * factor)
            total = jnp.sum(weights, axis=1, keepdims=True)
            mixed = jnp.dot(weights.astype(jnp.bfloat16), jnp.concatenate(v_parts, axis=0),
                            preferred_element_type=jnp.float32)
            att[h, rows, :] = (mixed / total).astype(jnp.bfloat16)

            @pl.when(step < tiles - 1)
            def _():
                a2a_copy(h, step + 1).start()
            return carry

        lax.fori_loop(0, tiles, one_tile, 0)
        own_rows = pl.ds(pl.multiple_of(z * TILE, TILE), TILE)
        own_columns = pl.ds(pl.multiple_of(z * HD, HD), HD)
        arecv[h, :, own_columns] = att[h, own_rows, :]

    block = 512

    def project(h):
        for s, ring in received:
            pair_copy(h, s, ring).wait_recv()
        for d in range(1, n_head):
            a2a_copy(h, d).wait_recv()
        lhs = arecv[h]
        for n in range(width // block):
            columns = slice(n * block, (n + 1) * block)
            rhs = wbuf[h, :, :, columns].reshape(n_head * HD, block)
            term = jnp.dot(lhs, rhs, preferred_element_type=jnp.float32)
            out[:, columns] = term if h == 0 else out[:, columns] + term

    def start_attend(h):
        for copy in far_copies(h) + core_copies(h):
            copy.wait_recv()
        for copy in own_kv(h):
            copy.wait()
        attend(h)

    pl.semaphore_wait(barrier, len(peers))
    for h in range(n_local - 1):
        for copy in far_copies(h):
            copy.start()
    tick(0)
    for h in range(n_local):
        for copy in core_copies(h):
            copy.start()
    own_q.wait()
    for step in ORDER:
        what, which = step
        if what == "tick":
            tick(which)
        elif what == "share":
            share(which)
        elif what == "far":
            for copy in far_copies(which):
                copy.start()
        elif what == "attend":
            start_attend(which)
        elif what == "project":
            project(which)
    for h in range(n_local):
        for copy in far_copies(h) + core_copies(h):
            copy.wait_send()
        for d in range(1, n_head):
            a2a_copy(h, d).wait_send()
        for s in range(hops):
            for ring in range(2):
                for copy in ring_copies(h, s, ring) + mate_copies(h, s, ring):
                    copy.wait_send()
        for s, ring in received:
            pair_copy(h, s, ring).wait_send()


ORDER = (
    ("tick", 1), ("tick", 2), ("far", 2), ("share", 0), ("tick", 3), ("share", 1), ("attend", 0), ("tick", 4),
    ("attend", 1), ("share", 2), ("share", 3), ("project", 0), ("attend", 2), ("project", 1), ("project", 2),
)


def by_tile(rows):
    return rows.reshape(rows.shape[0] // TILE, TILE, rows.shape[1])


def body(queries, key_rows, values, out_weight, gate_scale, window):
    n_tm, n_head = lax.axis_size("tm"), lax.axis_size("head")
    tokens, features = queries.shape
    n_local = features // HD
    width = out_weight.shape[1]
    hops = n_head // 2
    dma = pltpu.SemaphoreType.DMA
    hbm_spec = pl.BlockSpec(memory_space=pltpu.HBM)
    projected = pl.pallas_call(
        functools.partial(kernel, n_tm, n_head, n_local),
        out_shape=jax.ShapeDtypeStruct((tokens // n_head, width), jnp.float32),
        in_specs=[hbm_spec] * 4 + [pl.BlockSpec(memory_space=pltpu.SMEM)],
        out_specs=pl.BlockSpec(memory_space=pltpu.VMEM),
        scratch_shapes=[
            pltpu.VMEM((tokens, features), jnp.bfloat16),
            pltpu.VMEM((n_local, tokens, HD), jnp.bfloat16),
            pltpu.VMEM((n_local, TILE, n_head * HD), jnp.bfloat16),
            pltpu.VMEM((n_local, n_head, HD, width), jnp.bfloat16),
        ] + [pltpu.VMEM((3 * tokens // TILE, TILE, HD), jnp.bfloat16)] * (2 * n_local) + [
            dma((3 * n_local + 1,)),
            dma((2 * n_local,)), dma((2 * n_local,)), dma((2 * n_local,)), dma((2 * n_local,)),
            dma((n_local, n_head)), dma((n_local, n_head)),
            dma((n_local, hops, 2, 2)), dma((n_local, hops, 2, 2)),
            dma((n_local, hops, 2, 2)), dma((n_local, hops, 2, 2)),
            dma((n_local, hops, 2)), dma((n_local, hops, 2)),
        ],
        compiler_params=pltpu.CompilerParams(
            collective_id=0, has_side_effects=True, vmem_limit_bytes=VMEM_LIMIT << 20),
        name="attend_and_project",
    )(queries, by_tile(key_rows), by_tile(values), out_weight, window.transpose(2, 0, 1))
    return gate_scale[None, :] * projected


def solution(mesh):
    placed = (
        P(("prompt", "tm"), "head"),
        P(("prompt", "tm"), "head"),
        P(("prompt", "tm"), "head"),
        P("head", None),
        P("prompt"),
        P(("prompt", "tm"), None, None),
    )
    return jax.shard_map(
        body,
        mesh=mesh,
        in_specs=placed,
        out_specs=P(("prompt", "tm", "head"), None),
        check_vma=False,
    )
```

time: 120 us -> 95.8 us (0.80)
  Pallas kernels: 115 us -> 92.3 us
  local copies, waits for them, and re-layouts: 1.44 us -> 0.01 us
    pallas_call x1, Pallas kernels: 115 us -> 92.3 us  [body(): pl.pallas_call(functools.partial(kernel, n_tm, n_head, n_local), out_shap...]
    unnamed x3 -> x2, local copies, waits for them, and re-layouts: 1.44 us -> 0.01 us
where the time goes in v1:
time: 95.8 us; the launch traced here: 95.7 us
  Pallas kernels  92.3 us (96%)
  other arithmetic  3.36 us (4%)
    pallas_call x1, Pallas kernels, body(): pl.pallas_call(functools.partial(kernel, n_tm, n_head, n_local), out_shap...  92.3 us
    mul x1, other arithmetic, body(): return gate_scale[None, :] * projected  3.36 us

profile of v1, /device:TPU:1, one launch (start us, length us, event | category | flops | bytes accessed | tf_op | source)
XLA Modules:
  0.0 95.7 jit_solution(11122792555372778191)
XLA Ops:
  0.0 0.0 copy-start
  0.0 92.3 %attend_and_project.1 = f32[192,3072]{1,0:T(8,128)} custom-call(bf16[1536,384]{1,0:T(8,128)(2,1)} %q_hbm.1, bf16[8,192,384]{2,1,0:T(8,128)(2,1)} %bitcast.3, bf16[8,192,384]{2,1,0:T(8,128)(2,1)} %bitcast.4, bf16[384,3072]{1,0:T(8,128)(2,1)} %w_hbm.1, s32[3,8,8]{2,1,0:T(8,128)} %bitcast.5), custom_call_target="tpu_custom_call" | custom-call | tf_op jit(solution)/shard_map/attend_and_project/pallas_call | solution.py:278
  92.3 0.0 copy-done
  92.3 3.4 %broadcast_multiply_fusion = f32[192,3072]{1,0:T(8,128)} fusion(f32[192,3072]{1,0:T(8,128)} %attend_and_project.1, f32[3072]{0:T(1024)S(1)} %copy-done), kind=kLoop, calls=%fused_computation | loop fusion | flops 589824 | bytes 4730880 | tf_op jit(solution)/shard_map/mul | solution.py:300
Async XLA Ops:
  0.0 92.3 %copy-start = (f32[3072]{0:T(1024)S(1)}, f32[3072]{0:T(1024)}, u32[]{:S(2)}) copy-start(f32[3072]{0:T(1024)} %param.10) | copy-start | bytes 36868

commit v2 on v1

--- a/solution.py
+++ b/solution.py
@@ -20,10 +20,10 @@
 BUSY = 1
 
 
-def kernel(n_tm, n_head, n_local, q_hbm, k_hbm, v_hbm, w_hbm, window, out,
-           qbuf, att, arecv, wbuf, *rest):
+def kernel(n_tm, n_head, n_local, q_hbm, k_hbm, v_hbm, w_hbm, window, out_hbm,
+           qbuf, att, arecv, wbuf, out, *rest):
     kbufs, vbufs = rest[:n_local], rest[n_local:2 * n_local]
-    (loc_sem, halo_send, halo_recv, core_send, core_recv, a_send, a_recv,
+    (loc_sem, out_sem, halo_send, halo_recv, core_send, core_recv, a_send, a_recv,
      ring_send, ring_recv, mate_send, mate_recv, pair_send, pair_recv) = rest[2 * n_local:]
     tokens = q_hbm.shape[0]
     tiles = tokens // TILE
@@ -203,6 +203,10 @@
 
     block = 512
 
+    def out_copy(n):
+        columns = pl.ds(n * block, block)
+        return pltpu.make_async_copy(out.at[:, columns], out_hbm.at[:, columns], out_sem.at[n])
+
     def project(h):
         for s, ring in received:
             pair_copy(h, s, ring).wait_recv()
@@ -214,6 +218,8 @@
             rhs = wbuf[h, :, :, columns].reshape(n_head * HD, block)
             term = jnp.dot(lhs, rhs, preferred_element_type=jnp.float32)
             out[:, columns] = term if h == 0 else out[:, columns] + term
+            if h == n_local - 1:
+                out_copy(n).start()
 
     def start_attend(h):
         for copy in far_copies(h) + core_copies(h):
@@ -255,11 +261,13 @@
                     copy.wait_send()
         for s, ring in received:
             pair_copy(h, s, ring).wait_send()
+    for n in range(width // block):
+        out_copy(n).wait()
 
 
 ORDER = (
-    ("tick", 1), ("tick", 2), ("far", 2), ("share", 0), ("tick", 3), ("share", 1), ("attend", 0), ("tick", 4),
-    ("attend", 1), ("share", 2), ("share", 3), ("project", 0), ("attend", 2), ("project", 1), ("project", 2),
+    ("tick", 1), ("tick", 2), ("far", 2), ("share", 0), ("tick", 3), ("attend", 0), ("share", 1), ("tick", 4),
+    ("attend", 1), ("share", 2), ("share", 3), ("attend", 2), ("project", 0), ("project", 1), ("project", 2),
 )
 
 
@@ -279,14 +287,15 @@
         functools.partial(kernel, n_tm, n_head, n_local),
         out_shape=jax.ShapeDtypeStruct((tokens // n_head, width), jnp.float32),
         in_specs=[hbm_spec] * 4 + [pl.BlockSpec(memory_space=pltpu.SMEM)],
-        out_specs=pl.BlockSpec(memory_space=pltpu.VMEM),
+        out_specs=hbm_spec,
         scratch_shapes=[
             pltpu.VMEM((tokens, features), jnp.bfloat16),
             pltpu.VMEM((n_local, tokens, HD), jnp.bfloat16),
             pltpu.VMEM((n_local, TILE, n_head * HD), jnp.bfloat16),
             pltpu.VMEM((n_local, n_head, HD, width), jnp.bfloat16),
+            pltpu.VMEM((tokens // n_head, width), jnp.float32),
         ] + [pltpu.VMEM((3 * tokens // TILE, TILE, HD), jnp.bfloat16)] * (2 * n_local) + [
-            dma((3 * n_local + 1,)),
+            dma((3 * n_local + 1,)), dma((width // 512,)),
             dma((2 * n_local,)), dma((2 * n_local,)), dma((2 * n_local,)), dma((2 * n_local,)),
             dma((n_local, n_head)), dma((n_local, n_head)),
             dma((n_local, hops, 2, 2)), dma((n_local, hops, 2, 2)),

time: 95.8 us -> 93.1 us (0.972)
  Pallas kernels: 92.3 us -> 88.8 us
    pallas_call x1, Pallas kernels: 92.3 us -> 88.8 us  [body(): pl.pallas_call(functools.partial(kernel, n_tm, n_head, n_local), out_shap...]
where the time goes in v2:
time: 93.1 us; the launch traced here: 92.2 us
  Pallas kernels  88.8 us (95%)
  other arithmetic  3.36 us (4%)
    pallas_call x1, Pallas kernels, body(): pl.pallas_call(functools.partial(kernel, n_tm, n_head, n_local), out_shap...  88.8 us
    mul x1, other arithmetic, body(): return gate_scale[None, :] * projected  3.36 us

profile of v2, /device:TPU:1, one launch (start us, length us, event | category | flops | bytes accessed | tf_op | source)
XLA Modules:
  0.0 92.2 jit_solution(11310750601733324693)
XLA Ops:
  0.0 0.0 copy-start
  0.0 88.8 %attend_and_project.1 = f32[192,3072]{1,0:T(8,128)} custom-call(bf16[1536,384]{1,0:T(8,128)(2,1)} %q_hbm.1, bf16[8,192,384]{2,1,0:T(8,128)(2,1)} %bitcast.3, bf16[8,192,384]{2,1,0:T(8,128)(2,1)} %bitcast.4, bf16[384,3072]{1,0:T(8,128)(2,1)} %w_hbm.1, s32[3,8,8]{2,1,0:T(8,128)} %bitcast.5), custom_call_target="tpu_custom_call" | custom-call | tf_op jit(solution)/shard_map/attend_and_project/pallas_call | solution.py:286
  88.9 0.0 copy-done
  88.9 3.4 %broadcast_multiply_fusion = f32[192,3072]{1,0:T(8,128)} fusion(f32[192,3072]{1,0:T(8,128)} %attend_and_project.1, f32[3072]{0:T(1024)S(1)} %copy-done), kind=kLoop, calls=%fused_computation | loop fusion | flops 589824 | bytes 4730880 | tf_op jit(solution)/shard_map/mul | solution.py:309
Async XLA Ops:
  0.0 88.9 %copy-start = (f32[3072]{0:T(1024)S(1)}, f32[3072]{0:T(1024)}, u32[]{:S(2)}) copy-start(f32[3072]{0:T(1024)} %param.10) | copy-start | bytes 36868

commit v3 on v2

--- a/solution.py
+++ b/solution.py
@@ -164,7 +164,8 @@
         kbuf, vbuf = kbufs[h], vbufs[h]
 
         def one_tile(step, carry):
-            i = (z + 1 + step) % tiles
+            d = hops + (step + 1) // 2 * (1 - 2 * (step % 2))
+            i = (z + d) % tiles
             i_h, i_w = i // NTW, i % NTW
             rows = pl.ds(pl.multiple_of(i * TILE, TILE), TILE)
             bias = jnp.zeros((1, SLOTS * TILE), jnp.float32)
@@ -193,7 +194,7 @@
 
             @pl.when(step < tiles - 1)
             def _():
-                a2a_copy(h, step + 1).start()
+                a2a_copy(h, d).start()
             return carry
 
         lax.fori_loop(0, tiles, one_tile, 0)

time: 93.1 us -> 93.5 us (level)
  Pallas kernels: 88.8 us -> 90 us
    pallas_call x1, Pallas kernels: 88.8 us -> 90 us  [body(): pl.pallas_call(functools.partial(kernel, n_tm, n_head, n_local), out_shap...]
where the time goes in v3:
time: 93.5 us; the launch traced here: 93.3 us
  Pallas kernels  90 us (96%)
  other arithmetic  3.36 us (4%)
    pallas_call x1, Pallas kernels, body(): pl.pallas_call(functools.partial(kernel, n_tm, n_head, n_local), out_shap...  90 us
    mul x1, other arithmetic, body(): return gate_scale[None, :] * projected  3.36 us

profile of v3, /device:TPU:1, one launch (start us, length us, event | category | flops | bytes accessed | tf_op | source)
XLA Modules:
  0.0 93.3 jit_solution(16133485294520939857)
XLA Ops:
  0.0 0.0 copy-start
  0.0 90.0 %attend_and_project.1 = f32[192,3072]{1,0:T(8,128)} custom-call(bf16[1536,384]{1,0:T(8,128)(2,1)} %q_hbm.1, bf16[8,192,384]{2,1,0:T(8,128)(2,1)} %bitcast.3, bf16[8,192,384]{2,1,0:T(8,128)(2,1)} %bitcast.4, bf16[384,3072]{1,0:T(8,128)(2,1)} %w_hbm.1, s32[3,8,8]{2,1,0:T(8,128)} %bitcast.5), custom_call_target="tpu_custom_call" | custom-call | tf_op jit(solution)/shard_map/attend_and_project/pallas_call | solution.py:287
  90.0 0.0 copy-done
  90.0 3.4 %broadcast_multiply_fusion = f32[192,3072]{1,0:T(8,128)} fusion(f32[192,3072]{1,0:T(8,128)} %attend_and_project.1, f32[3072]{0:T(1024)S(1)} %copy-done), kind=kLoop, calls=%fused_computation | loop fusion | flops 589824 | bytes 4730880 | tf_op jit(solution)/shard_map/mul | solution.py:310
Async XLA Ops:
  0.0 90.0 %copy-start = (f32[3072]{0:T(1024)S(1)}, f32[3072]{0:T(1024)}, u32[]{:S(2)}) copy-start(f32[3072]{0:T(1024)} %param.10) | copy-start | bytes 36868
